TPU v7x, 32 devices: a whole 2x2x4 slice. The times are simulated.
32 devices in a mesh: sta: 8 (over z, x), seg: 4 (over y, core).
Axes of the slice: x: 2, y: 2, z: 4, core: 2. Of those that a mesh axis runs over, the one named last changes fastest.
Arguments:
- records: bfloat16 [128, 32, 4096], P('sta', 'seg'), may hold values from -6 to 6
- fir_taps: bfloat16 [32], replicated, may hold values from -1 to 1
- counts: int32 [128], replicated, may hold values from 1 to 32
- pair_blocks: int32 [16, 2], replicated, may hold values from 0 to 7, as said below
- owners: int32 [16, 1], replicated, may hold values from 0 to 7; in each aligned block of 16 rows (0 to 15, 16 to 31, ...) at most 4 rows name the same one
Outputs:
- correlation: float32 [32, 512, 256], P('sta', None, 'seg')
Inputs may be any that keep to these rules, and one draw needn't show every extreme that they name: `pair_blocks`: each row names two station blocks at most one step apart in row and in column of a grid 8 blocks wide (block = 8 * row + column); every block is the first of exactly two rows. `owners`: every owner is named by 1 to 4 rows, a bound that some block reaches. A station's record is valid in segments 0 to counts - 1.
All inputs are finite; a program needn't handle non-finite values.
Results may differ from a plain program's by a relative error of at most 0.0089.
Values may be sent and summed in bfloat16 or wider, within the bound.
A program may use at most 192 MiB of HBM per device.

v0:
```python
import math

import jax
import jax.numpy as jnp
from jax import lax
from jax.sharding import PartitionSpec as P

DEC = 4
TAPS = 32
NLAG = 512
CAP = 4


WATER = 0.1
TINY = 1e-06


def forward_table(seglen):
    sample_pos = jnp.arange(seglen, dtype=jnp.int32)
    freq_pos = jnp.arange(seglen // 2, dtype=jnp.int32)
    phase = sample_pos[:, None] * freq_pos[None, :] % seglen
    angle = phase.astype(jnp.float32) * (2.0 * math.pi / seglen)
    return jnp.concatenate([jnp.cos(angle), -jnp.sin(angle)], axis=1).astype(jnp.bfloat16)


def inverse_table(seglen, nlag):
    freq_pos = jnp.arange(seglen // 2, dtype=jnp.int32)
    lag_pos = jnp.arange(nlag, dtype=jnp.int32) - nlag // 2
    phase = jnp.mod(freq_pos[:, None] * lag_pos[None, :], seglen)
    angle = phase.astype(jnp.float32) * (2.0 * math.pi / seglen)
    scale = 1.0 / math.sqrt(seglen // 2)
    both = jnp.stack([jnp.cos(angle) * scale, -jnp.sin(angle) * scale], axis=1)
    return both.reshape(seglen, nlag).astype(jnp.bfloat16)


def whiten(spectrum, nfreq):
    real_part = spectrum[:, :nfreq]
    imag_part = spectrum[:, nfreq:]
    magnitude = jnp.sqrt(real_part * real_part + imag_part * imag_part)
    mean_level = jnp.mean(magnitude, axis=1, keepdims=True)
    divisor = magnitude + WATER * mean_level + TINY
    return spectrum / jnp.concatenate([divisor, divisor], axis=1)


def fir_matrix(fir_taps):
    window_pos = jnp.arange(128 + 128 * DEC, dtype=jnp.int32)
    out_pos = jnp.arange(128, dtype=jnp.int32)
    tap_of = DEC * out_pos[None, :] + DEC - 1 + 128 - window_pos[:, None]
    inside = (tap_of >= 0) & (tap_of < TAPS)
    looked = jnp.take(fir_taps.astype(jnp.float32), jnp.clip(tap_of, 0, TAPS - 1))
    return jnp.where(inside, looked, 0.0).astype(jnp.bfloat16)


def slot_tables(pair_blocks, owners, sta_count):
    owner_ids = owners[:, 0]
    position = jnp.arange(owner_ids.shape[0], dtype=jnp.int32)
    same_owner = (owner_ids[:, None] == owner_ids[None, :]) & (
        position[None, :] < position[:, None]
    )
    rank_of = jnp.sum(same_owner.astype(jnp.int32), axis=1)
    slot_of = owner_ids * CAP + rank_of
    slot_hit = slot_of[None, :] == jnp.arange(sta_count * CAP, dtype=jnp.int32)[:, None]
    first_block = jnp.sum(jnp.where(slot_hit, pair_blocks[None, :, 0], 0), axis=1)
    second_block = jnp.sum(jnp.where(slot_hit, pair_blocks[None, :, 1], 0), axis=1)
    live_mask = jnp.any(slot_hit, axis=1).astype(jnp.float32)
    return (first_block, second_block, live_mask)


def cross_spectra(left_real, left_imag, right_real, right_imag, form):
    real_sum = jnp.einsum(form, left_real, right_real, preferred_element_type=jnp.float32)
    real_sum = real_sum + jnp.einsum(
        form, left_imag, right_imag, preferred_element_type=jnp.float32
    )
    imag_sum = jnp.einsum(form, left_imag, right_real, preferred_element_type=jnp.float32)
    imag_sum = imag_sum - jnp.einsum(
        form, left_real, right_imag, preferred_element_type=jnp.float32
    )
    return (real_sum, imag_sum)


def local(records, fir_taps, counts, pair_blocks, owners):
    block_size, seg_local, raw_length = records.shape
    sta_count = lax.axis_size("sta")
    seg_count = lax.axis_size("seg")
    seglen = raw_length // DEC
    nfreq = seglen // 2
    band_width = nfreq // sta_count
    row_count = block_size * seg_local
    nblocks = seglen // 128
    framed = records.reshape(row_count, nblocks, 128 * DEC)
    tails = jnp.concatenate(
        [jnp.zeros((row_count, 1, 128), jnp.bfloat16), framed[:, :-1, -128:]], axis=1
    )
    window = jnp.concatenate([tails, framed], axis=2)
    decimated = jnp.einsum(
        "rbw,wn->rbn", window, fir_matrix(fir_taps), preferred_element_type=jnp.float32
    )
    samples = decimated.reshape(row_count, seglen).astype(jnp.bfloat16)
    spectrum = jnp.dot(samples, forward_table(seglen), preferred_element_type=jnp.float32)
    white = whiten(spectrum, nfreq)
    sta_index = lax.axis_index("sta")
    seg_index = lax.axis_index("seg")
    local_counts = lax.dynamic_slice_in_dim(counts, sta_index * block_size, block_size)
    seg_ids = seg_index * seg_local + jnp.arange(seg_local, dtype=jnp.int32)
    valid = (seg_ids[None, :] < local_counts[:, None]).astype(jnp.float32).reshape(row_count, 1)
    whitened = (white * valid).astype(jnp.bfloat16)
    first_block, second_block, live_mask = slot_tables(pair_blocks, owners, sta_count)
    pair_count = block_size * block_size
    counts_grid = counts.reshape(sta_count, block_size)
    common = jnp.minimum(
        counts_grid[first_block][:, :, None], counts_grid[second_block][:, None, :]
    )
    factor = live_mask[:, None] / common.astype(jnp.float32).reshape(sta_count * CAP, pair_count)
    lane_width = pair_count // seg_count
    outgoing = whitened.reshape(block_size, seg_local, 2, sta_count, band_width)
    outgoing = outgoing.transpose(3, 4, 2, 1, 0).reshape(
        sta_count, band_width, 2, seg_local * block_size
    )
    bands = lax.all_to_all(outgoing, "sta", split_axis=0, concat_axis=0, tiled=True)
    bands = bands.reshape(sta_count, band_width, 2, seg_local, block_size)
    left = bands[first_block]
    right = bands[second_block]
    real_sum, imag_sum = cross_spectra(
        left[:, :, 0], left[:, :, 1], right[:, :, 0], right[:, :, 1], "qfsi,qfsj->qfij"
    )
    cross = jnp.stack([real_sum, imag_sum], axis=2) * live_mask[:, None, None, None, None]
    cross = cross.reshape(sta_count, CAP, band_width, 2, pair_count)
    moved = lax.all_to_all(cross, "sta", split_axis=0, concat_axis=2, tiled=True)
    summed = lax.psum_scatter(moved, "seg", scatter_dimension=4, tiled=True)[0]
    own_factor = lax.dynamic_slice(
        factor, (sta_index * CAP, seg_index * lane_width), (CAP, lane_width)
    )
    stacked = (summed * own_factor[:, None, None, :]).astype(jnp.bfloat16)
    inv_table = inverse_table(seglen, NLAG)
    stacked = stacked.reshape(CAP, 2 * nfreq, lane_width)
    return jnp.einsum("kl,ckp->clp", inv_table, stacked, preferred_element_type=jnp.float32)


def solution(mesh):
    in_specs = (P("sta", "seg", None), P(), P(), P(), P())
    out_specs = P("sta", None, "seg")
    return jax.shard_map(local, mesh=mesh, in_specs=in_specs, out_specs=out_specs, check_vma=False)
```

profile of v0, /device:TPU:0, one launch (start us, length us, event | category | flops | bytes accessed | tf_op | source)
XLA Modules:
  0.0 368.3 jit_solution(3275517761861010827)
XLA Ops:
  6.5 2.1 fusion.245
  8.6 1.8 fusion.246
  10.4 8.5 %negate_convert_fusion = (bf16[1024,512]{1,0:T(8,128)(2,1)S(1)}, bf16[1024,512]{1,0:T(8,128)(2,1)S(1)}) fusion(), kind=kLoop, calls=%fused_computation.29 | loop fusion | flops 8912896 | bytes 2097152 | tf_op jit(solution)/shard_map/convert.5
  19.0 1.6 copy.99
  21.0 21.4 %fusion.27 = bf16[128,8,128]{0,2,1:T(8,128)(2,1)S(1)} fusion(bf16[128,7,128]{2,0,1:T(8,128)(2,1)S(1)} %slice.77, bf16[128,8,512]{2,0,1:T(8,128)(2,1)S(1)} %copy.75, bf16[]{:T(256)} %bitcast.50, bf16[]{:T(256)} %bitcast.51, bf16[]{:T(256)} %bitcast.52, bf16[]{:T(256)} %bitcast.53, bf16[]{:T(256)} %bitcast.54, bf16[]{:T(256)} %bitcast.56, bf16[]{:T(256)} %bitcast.55, ...), kind=kOutput, calls=%fused_computation.43 | convolution fusion | flops 178388992 | bytes 1540672 | tf_op jit(solution)/shard_map/rbw,wn->rbn/dot_general | solution.py:95
  45.2 7.3 %all-to-all-start = ((bf16[8,64,2,128]{3,1,2,0:T(8,128)(2,1)}), bf16[8,64,2,128]{3,1,2,0:T(8,128)(2,1)S(1)}, u32[]{:S(2)}, u32[]{:S(2)}) async-start(bf16[8,64,2,128]{3,1,2,0:T(8,128)(2,1)} %copy.78), calls=%async_computation | async-start | bytes 524288 | tf_op jit(solution)/shard_map/all_to_all | solution.py:119
  53.2 8.2 %all-to-all-done = bf16[8,64,2,128]{3,1,2,0:T(8,128)(2,1)S(1)} async-done(((bf16[8,64,2,128]{3,1,2,0:T(8,128)(2,1)}), bf16[8,64,2,128]{3,1,2,0:T(8,128)(2,1)S(1)}, u32[]{:S(2)}, u32[]{:S(2)}) %all-to-all-start) | async-done | bytes 262176 | tf_op jit(solution)/shard_map/all_to_all | solution.py:119
  61.7 1.0 gather_fusion.1
  62.6 1.7 fusion.244
  64.3 4.8 %copy.96 = bf16[32,64,1,8,16]{4,3,1,0,2:T(8,128)(2,1)} copy(bf16[32,64,1,8,16]{1,4,3,2,0:T(8,128)(2,1)} %get-tuple-element.10) | data formatting | bytes 1048576
  69.1 0.9 gather_fusion
  70.1 1.7 fusion.243
  71.8 5.0 %copy.95 = bf16[32,64,1,8,16]{4,3,1,0,2:T(8,128)(2,1)} copy(bf16[32,64,1,8,16]{1,4,3,2,0:T(8,128)(2,1)} %get-tuple-element.7) | data formatting | bytes 1048576
  76.8 3.5 copy.98
  80.3 3.5 copy.97
  83.8 10.3 %fusion.6 = f32[32,64,16,16]{3,2,1,0:T(8,128)} fusion(bf16[32,64,1,8,16]{4,3,1,0,2:T(8,128)(2,1)} %copy.96, bf16[32,64,1,8,16]{4,3,1,0,2:T(8,128)(2,1)} %copy.95), kind=kOutput, calls=%fused_computation.13 | convolution fusion | flops 8388608 | bytes 3145728 | tf_op jit(solution)/shard_map/qfsi,qfsj->qfij/dot_general | solution.py:70
  94.1 6.9 %fusion.2 = f32[32,64,16,16]{3,2,1,0:T(8,128)} fusion(bf16[32,64,1,8,16]{4,3,1,0,2:T(8,128)(2,1)S(1)} %copy-done.1, bf16[32,64,1,8,16]{4,3,1,0,2:T(8,128)(2,1)S(1)} %copy-done), kind=kOutput, calls=%fused_computation.9 | convolution fusion | flops 8388608 | bytes 3145728 | tf_op jit(solution)/shard_map/qfsi,qfsj->qfij/dot_general | solution.py:74
  101.0 13.1 %convolution_add_fusion = f32[32,64,16,16]{3,2,1,0:T(8,128)} fusion(f32[32,64,16,16]{3,2,1,0:T(8,128)} %fusion.6, bf16[32,64,1,8,16]{4,3,1,0,2:T(8,128)(2,1)} %copy.98, bf16[32,64,1,8,16]{4,3,1,0,2:T(8,128)(2,1)S(1)} %copy-done.1), kind=kOutput, calls=%fused_computation.5 | convolution fusion | flops 8912896 | bytes 5242880 | tf_op jit(solution)/shard_map/qfsi,qfsj->qfij/dot_general | solution.py:71
  114.1 11.9 %copy.84 = f32[32,64,16,16]{1,3,2,0:T(8,128)} copy(f32[32,64,16,16]{3,2,1,0:T(8,128)} %convolution_add_fusion) | data formatting | bytes 4194304 | tf_op jit(solution)/shard_map/add | solution.py:71
  126.0 15.7 %convolution_subtract_fusion = f32[32,64,16,16]{3,2,1,0:T(8,128)} fusion(f32[32,64,16,16]{3,2,1,0:T(8,128)} %fusion.2, bf16[32,64,1,8,16]{4,3,1,0,2:T(8,128)(2,1)} %copy.98, bf16[32,64,1,8,16]{4,3,1,0,2:T(8,128)(2,1)} %copy.95), kind=kOutput, calls=%fused_computation.4 | convolution fusion | flops 8912896 | bytes 5242880 | tf_op jit(solution)/shard_map/qfsi,qfsj->qfij/dot_general | solution.py:75
  141.7 11.9 %copy.85 = f32[32,64,16,16]{1,3,2,0:T(8,128)} copy(f32[32,64,16,16]{3,2,1,0:T(8,128)} %convolution_subtract_fusion) | data formatting | bytes 4194304 | tf_op jit(solution)/shard_map/sub | solution.py:75
  153.6 8.3 %maximum_multiply_fusion = f32[8,4,64,2,256]{2,4,1,0,3:T(8,128)} fusion(f32[8,4,64,1,256]{2,4,1,0,3:T(8,128)} %bitcast.315, f32[8,4,64,1,256]{2,4,1,0,3:T(8,128)} %bitcast.314, f32[8,4]{1,0:T(8,128)S(1)} %reshape.295), kind=kLoop, calls=%fused_computation.6 | loop fusion | flops 2097152 | bytes 8388736 | tf_op jit(solution)/shard_map/mul | solution.py:126
  161.9 6.8 %copy.86 = f32[8,4,64,2,256]{4,2,3,1,0:T(8,128)} copy(f32[8,4,64,2,256]{2,4,1,0,3:T(8,128)} %maximum_multiply_fusion) | data formatting | bytes 8388608 | tf_op jit(solution)/shard_map/mul | solution.py:126
  168.7 96.6 %all_to_all.23 = f32[8,4,64,2,256]{4,2,3,1,0:T(8,128)S(1)} all-to-all(f32[8,4,64,2,256]{4,2,3,1,0:T(8,128)} %copy.86), channel_id=1, replica_groups=mesh['sta'=8,'seg'=4] {'sta'}, dimensions={0} | all-to-all | bytes 8388608 | tf_op jit(solution)/shard_map/all_to_all | solution.py:128
  265.4 2.3 copy.87
  267.6 5.6 %copy.88 = f32[1,4,512,2,256]{2,1,3,0,4:T(4,128)} copy(f32[1,4,512,2,256]{4,2,3,1,0:T(8,128)} %bitcast.316) | data formatting | bytes 8388608 | tf_op jit(solution)/shard_map/all_to_all | solution.py:128
  274.7 4.5 %multiply_convert_fusion.1 = (bf16[512,1,512]{2,0,1:T(8,128)(2,1)S(1)}, bf16[512,1,512]{2,0,1:T(8,128)(2,1)S(1)}) fusion(s32[512]{0:T(512)S(1)} %iota_add_fusion), kind=kLoop, calls=%fused_computation.51 | loop fusion | flops 4980736 | bytes 1050624 | tf_op jit(solution)/shard_map/convert.2
  279.3 1.1 copy.92
  282.2 75.5 %all-reduce.4.cloned.1.call-done = f32[1,4,512,2,256]{2,1,3,0,4:T(4,128)} async-done(((f32[1,4,512,2,256]{2,1,3,0,4:T(4,128)}), f32[1,4,512,2,256]{2,1,3,0,4:T(4,128)}) %all-reduce.4.cloned.1.call-update) | async-done | bytes 4194320
  357.7 1.5 fusion.33
  359.1 1.0 copy.91
  360.1 1.3 convolution_bitcast_fusion
  (56 shorter events, 6.8 us)
Async XLA Ops:
  42.4 0.8 copy-start.5
  42.4 10.3 %copy-start.4 = (s32[16,2]{0,1:T(2,128)S(1)}, s32[16,2]{0,1:T(2,128)}, u32[]{:S(2)}) copy-start(s32[16,2]{0,1:T(2,128)} %param.8) | copy-start | bytes 388
  42.4 10.3 %copy-start.6 = (s32[16,1]{0,1:T(1,128)S(1)}, s32[16,1]{0,1:T(1,128)}, u32[]{:S(2)}) copy-start(s32[16,1]{0,1:T(1,128)} %param.9) | copy-start | bytes 196
  45.2 16.2 %all-to-all-start = ((bf16[8,64,2,128]{3,1,2,0:T(8,128)(2,1)}), bf16[8,64,2,128]{3,1,2,0:T(8,128)(2,1)S(1)}, u32[]{:S(2)}, u32[]{:S(2)}) async-start(bf16[8,64,2,128]{3,1,2,0:T(8,128)(2,1)} %copy.78), calls=%async_computation | async-start | bytes 524288 | tf_op jit(solution)/shard_map/all_to_all | solution.py:119
  52.4 305.2 %all-reduce.4.cloned.1.call-start = ((), (), s32[]{:S(2)}) async-start(), calls=%async_computation.2 | async-start | bytes 8388608
  71.8 5.0 %copy-start.2 = (bf16[32,64,1,8,16]{1,4,3,2,0:T(8,128)(2,1)S(1)}, bf16[32,64,1,8,16]{1,4,3,2,0:T(8,128)(2,1)}, u32[]{:S(2)}) copy-start(bf16[32,64,1,8,16]{1,4,3,2,0:T(8,128)(2,1)} %get-tuple-element.9) | copy-start | bytes 1572868
  71.8 8.5 %copy-start.3 = (bf16[32,64,1,8,16]{1,4,3,2,0:T(8,128)(2,1)S(1)}, bf16[32,64,1,8,16]{1,4,3,2,0:T(8,128)(2,1)}, u32[]{:S(2)}) copy-start(bf16[32,64,1,8,16]{1,4,3,2,0:T(8,128)(2,1)} %get-tuple-element.8) | copy-start | bytes 1572868
  83.8 10.3 %copy-start = (bf16[32,64,1,8,16]{4,3,1,0,2:T(8,128)(2,1)S(1)}, bf16[32,64,1,8,16]{4,3,1,0,2:T(8,128)(2,1)}, u32[]{:S(2)}) copy-start(bf16[32,64,1,8,16]{4,3,1,0,2:T(8,128)(2,1)} %copy.96) | copy-start | bytes 1572868
  83.8 10.3 %copy-start.1 = (bf16[32,64,1,8,16]{4,3,1,0,2:T(8,128)(2,1)S(1)}, bf16[32,64,1,8,16]{4,3,1,0,2:T(8,128)(2,1)}, u32[]{:S(2)}) copy-start(bf16[32,64,1,8,16]{4,3,1,0,2:T(8,128)(2,1)} %copy.97) | copy-start | bytes 1572868
  273.2 7.6 %copy-start.7 = (u32[32]{0:T(128)S(1)}, u32[32]{0:T(128)}, u32[]{:S(2)}) copy-start(u32[32]{0:T(128)} %constant.131) | copy-start | bytes 388
Sparse Core Ops, SparseCore 0:
  273.3 84.2 all-reduce.3
where the time goes:
time: 369 us; the launch traced here: 368 us
  blocking collectives  96.6 us (26%)
  waiting for transfers between devices  83.7 us (23%)
  local copies, waits for them, and re-layouts  73.2 us (20%)
  matrix products  69.1 us (19%)
  other arithmetic  23.9 us (6%)
  between operations  14.4 us (4%)
  starting transfers between devices  7.47 us (2%)
    all_to_all x1, blocking collectives, local(): lax.all_to_all(cross, 'sta', split_axis=0, concat_axis=2, tiled=True)  96.6 us
    unnamed x2, waiting for transfers between devices  75.5 us
    dot_general x1, matrix products, local(): jnp.einsum('rbw,wn->rbn', window, fir_matrix(fir_taps), preferred_element...  21.4 us
    unnamed x22, local copies, waits for them, and re-layouts  19.1 us
    dot_general x1, matrix products, cross_spectra(): jnp.einsum(form, left_real, right_imag, preferred_element_type=jnp.float32)  15.7 us
    dot_general x1, matrix products, cross_spectra(): jnp.einsum(form, left_imag, right_imag, preferred_element_type=jnp.float32)  13.1 us
    another operation x2, other arithmetic  13 us
    sub x1, local copies, waits for them, and re-layouts, cross_spectra(): imag_sum - jnp.einsum(form, left_real, right_imag, preferred_element_type...  11.9 us
  transfers between devices with their start and end apart: 2, of which 2 were waited for; matrix products, arithmetic and copies ran while one was open for 2% of the time, Pallas kernels for 0%

commit v1 on v0

v1 whole, which is shorter than its diff:
```python
import functools
import math

import jax
import jax.numpy as jnp
import ml_dtypes
import numpy as np
from jax import lax
from jax.experimental import pallas as pl
from jax.experimental.pallas import tpu as pltpu
from jax.sharding import PartitionSpec as P

DEC = 4
TAPS = 32
NLAG = 512
CAP = 4
WATER = 0.1
TINY = 1e-06
AXES = ("sta", "seg")
VMEM = pl.BlockSpec(memory_space=pltpu.VMEM)
SMEM = pl.BlockSpec(memory_space=pltpu.SMEM)
LIMIT = 50 * 2**20


def forward_rows(seglen):
    phase = np.arange(seglen // 2)[:, None] * np.arange(seglen)[None, :] % seglen
    angle = phase * (2.0 * math.pi / seglen)
    both = np.concatenate([np.cos(angle), -np.sin(angle)], axis=0)
    return both.astype(np.float32).astype(ml_dtypes.bfloat16)


def inverse_rows(seglen, nlag, width):
    nfreq = seglen // 2
    lag = np.arange(nlag) - nlag // 2
    angle = (lag[:, None] * np.arange(nfreq)[None, :] % seglen) * (2.0 * math.pi / seglen)
    scale = 1.0 / math.sqrt(nfreq)
    both = np.stack([np.cos(angle) * scale, -np.sin(angle) * scale], axis=1)
    both = both.reshape(nlag, 2, nfreq // width, width).transpose(0, 2, 1, 3)
    return both.reshape(nlag, 2 * nfreq).astype(np.float32).astype(ml_dtypes.bfloat16)


def spread_tables(block, segs):
    eye = np.einsum("ai,sz->aszi", np.eye(block), np.eye(segs)).reshape(block * segs, segs, block)
    by_i = np.broadcast_to(eye[..., None], eye.shape + (block,))
    by_j = np.broadcast_to(eye[:, :, None, :], eye.shape[:2] + (block, block))
    shape = (block * segs, segs * block * block)
    return tuple(t.reshape(shape).astype(ml_dtypes.bfloat16) for t in (by_i, by_j))


def front_kernel(block, segs, taps_ref, counts_ref, rec_ref, dft_ref, out_ref, samp_ref):
    rows = block * segs
    nblocks = rec_ref.shape[1] // (128 * DEC)
    nfreq = dft_ref.shape[0] // 2
    span = 128 * DEC
    out_pos = lax.broadcasted_iota(jnp.int32, (128, 128 + span), 0)
    window_pos = lax.broadcasted_iota(jnp.int32, (128, 128 + span), 1)
    tap_of = DEC * out_pos + DEC - 1 + 128 - window_pos
    fir = jnp.zeros((128, 128 + span), jnp.float32)
    for k in range(TAPS):
        fir = jnp.where(tap_of == k, taps_ref[k], fir)
    fir = fir.astype(jnp.bfloat16)
    for b in range(nblocks):
        low = max(b * span - 128, 0)
        window = rec_ref[:, low : (b + 1) * span]
        kept = fir if b else fir[:, 128:]
        dec = lax.dot_general(
            kept, window, (((1,), (1,)), ((), ())), preferred_element_type=jnp.float32
        )
        samp_ref[b * 128 : (b + 1) * 128, :] = dec.astype(jnp.bfloat16)
    spectrum = jnp.dot(dft_ref[...], samp_ref[...], preferred_element_type=jnp.float32)
    real, imag = spectrum[:nfreq], spectrum[nfreq:]
    magnitude = jnp.sqrt(real * real + imag * imag)
    mean_level = jnp.sum(magnitude, axis=0, keepdims=True) * (1.0 / nfreq)
    divisor = magnitude + WATER * mean_level + TINY
    lane = lax.broadcasted_iota(jnp.int32, (1, rows), 1)
    first = lax.axis_index("sta") * block
    limit = jnp.zeros((1, rows), jnp.int32)
    for i in range(block):
        limit = jnp.where(lane // segs == i, counts_ref[first + i], limit)
    valid = (lax.axis_index("seg") * segs + lane % segs < limit).astype(jnp.float32)
    out_real = (real / divisor * valid).astype(jnp.bfloat16)
    out_imag = (imag / divisor * valid).astype(jnp.bfloat16)
    if len(out_ref.shape) == 2:
        out_ref[:nfreq, :] = out_real
        out_ref[nfreq:, :] = out_imag
    else:
        width = out_ref.shape[1] // 2
        for d in range(out_ref.shape[0]):
            out_ref[d, :width, :] = out_real[d * width : (d + 1) * width]
            out_ref[d, width:, :] = out_imag[d * width : (d + 1) * width]


def cross_kernel(
    groups, segs, owners_ref, pairs_ref, counts_ref, band_ref, by_i_ref, by_j_ref,
    out_ref, left_ref, right_ref, made_ref, slot_ref, used_ref,
):
    npairs = owners_ref.shape[0]
    nslots = slot_ref.shape[0]
    nsta = used_ref.shape[0]
    block = counts_ref.shape[0] // nsta
    lanes = block * block
    width = band_ref.shape[1] // 2

    @pl.loop(0, nslots)
    def _(q):
        slot_ref[q] = -1

    @pl.loop(0, nsta)
    def _(o):
        used_ref[o] = 0

    @pl.loop(0, npairs)
    def _(p):
        owner = owners_ref[p, 0]
        slot_ref[owner * CAP + used_ref[owner]] = p
        used_ref[owner] = used_ref[owner] + 1

    @pl.loop(0, nsta)
    def _(b):
        held = band_ref[pl.ds(b * groups, groups)].reshape(groups * 2 * width, -1)
        for s in range(segs):
            cols = slice(s * lanes, (s + 1) * lanes)
            for table, into in ((by_i_ref, left_ref), (by_j_ref, right_ref)):
                wide = jnp.dot(held, table[:, cols], preferred_element_type=jnp.float32)
                into[b, s] = wide

    lane = lax.broadcasted_iota(jnp.int32, (1, lanes), 1)
    low = lax.broadcasted_iota(jnp.int32, (2 * width, 128), 1) < 64

    @pl.loop(0, nslots // 2)
    def _(t):
        for e in range(2):
            pair = slot_ref[2 * t + e]

            @pl.when(pair < 0)
            def _():
                made_ref[e] = jnp.zeros(made_ref.shape[1:], jnp.float32)

            @pl.when(pair >= 0)
            def _():
                first, second = pairs_ref[pair, 0], pairs_ref[pair, 1]
                real = jnp.zeros((width, lanes), jnp.float32)
                imag = jnp.zeros((width, lanes), jnp.float32)
                for s in range(segs):
                    for g in range(groups):
                        at = g * 2 * width
                        lr = left_ref[first, s, at : at + width, :]
                        li = left_ref[first, s, at + width : at + 2 * width, :]
                        rr = right_ref[second, s, at : at + width, :]
                        ri = right_ref[second, s, at + width : at + 2 * width, :]
                        real = real + lr * rr + li * ri
                        imag = imag + li * rr - lr * ri
                left_count = jnp.zeros((1, lanes), jnp.int32)
                right_count = jnp.zeros((1, lanes), jnp.int32)
                for i in range(block):
                    left_count = jnp.where(lane // block == i, counts_ref[first * block + i], left_count)
                    right_count = jnp.where(lane % block == i, counts_ref[second * block + i], right_count)
                factor = 1.0 / jnp.minimum(left_count, right_count).astype(jnp.float32)
                made_ref[e, :width] = real * factor
                made_ref[e, width:] = imag * factor

        owner, half = t // (CAP // 2), t % (CAP // 2)
        parts = lanes // 64
        for j in range(parts):
            cols = slice(j // 2 * 128, j // 2 * 128 + 128)
            zero, one = made_ref[0, :, cols], made_ref[1, :, cols]
            if j % 2:
                zero = pltpu.roll(zero, 64, 1)
            else:
                one = pltpu.roll(one, 64, 1)
            out_ref[owner * parts + j, half] = jnp.where(low, zero, one).astype(jnp.bfloat16)


def cross_plain(bands, counts, pair_blocks, owners, nsta, groups, segs, width):
    owner_ids = owners[:, 0]
    position = jnp.arange(owner_ids.shape[0], dtype=jnp.int32)
    same = (owner_ids[:, None] == owner_ids[None, :]) & (position[None, :] < position[:, None])
    slot_of = owner_ids * CAP + jnp.sum(same.astype(jnp.int32), axis=1)
    block = counts.shape[0] // nsta
    hit = (slot_of[:, None] == jnp.arange(nsta * CAP, dtype=jnp.int32)[None, :]).astype(jnp.bfloat16)
    blocks = jnp.arange(nsta, dtype=jnp.int32)
    data = bands.reshape(nsta, groups, 2, width, block, segs)
    grid = counts.reshape(nsta, block).astype(jnp.float32)
    sides, limits = [], []
    for side in range(2):
        pick = (pair_blocks[:, side][:, None] == blocks[None, :]).astype(jnp.bfloat16)
        chosen = jnp.einsum("pn,ngufis->pgufis", pick, data, preferred_element_type=jnp.float32)
        sides.append(chosen.astype(jnp.bfloat16))
        limits.append(jnp.sum(jnp.where(pick[:, :, None] > 0, grid[None], 0.0), axis=1))
    left, right = sides
    common = jnp.minimum(limits[0][:, None, :, None], limits[1][:, None, None, :])
    dot = functools.partial(jnp.einsum, "pgfis,pgfjs->pfij", preferred_element_type=jnp.float32)
    real = dot(left[:, :, 0], right[:, :, 0]) + dot(left[:, :, 1], right[:, :, 1])
    imag = dot(left[:, :, 1], right[:, :, 0]) - dot(left[:, :, 0], right[:, :, 1])
    made = jnp.stack([real / common, imag / common], axis=1).astype(jnp.bfloat16)
    slots = jnp.einsum("pq,pufl->qufl", hit, made.reshape(made.shape[:3] + (block * block,)), preferred_element_type=jnp.float32)
    slots = slots.astype(jnp.bfloat16).reshape(nsta, CAP, 2, width, groups, block * block // groups)
    return slots.transpose(0, 4, 2, 3, 1, 5).reshape(nsta * groups, 2 * width, CAP * block * block // groups)


def last_kernel(inv_ref, stack_ref, out_ref):
    result = jnp.dot(inv_ref[...], stack_ref[...], preferred_element_type=jnp.float32)
    lanes = out_ref.shape[2]
    for c in range(out_ref.shape[0]):
        out_ref[c] = result[:, c * lanes : (c + 1) * lanes]


def last_kernel_halves(inv_ref, stack_ref, out_ref):
    for h in range(stack_ref.shape[1]):
        held = stack_ref[:, h].reshape(-1, 128)
        result = jnp.dot(inv_ref[...], held, preferred_element_type=jnp.float32)
        out_ref[2 * h] = result[:, :64]
        out_ref[2 * h + 1] = result[:, 64:]


def local(records, fir_taps, counts, pair_blocks, owners):
    block, segs, raw = records.shape
    nsta, groups = lax.axis_size("sta"), lax.axis_size("seg")
    devices = nsta * groups
    seglen = raw // DEC
    nfreq = seglen // 2
    width = nfreq // devices
    rows = block * segs
    lanes = block * block
    params = pltpu.CompilerParams(vmem_limit_bytes=LIMIT)
    fast = width % 16 == 0 and lanes // groups == 64 and rows == 128
    bf16 = jnp.bfloat16

    shape = (devices, 2 * width, rows) if fast else (2 * nfreq, rows)
    white = pl.pallas_call(
        functools.partial(front_kernel, block, segs),
        out_shape=jax.ShapeDtypeStruct(shape, bf16),
        in_specs=[SMEM, SMEM, VMEM, VMEM],
        out_specs=VMEM,
        scratch_shapes=[pltpu.VMEM((seglen, rows), bf16)],
        compiler_params=params,
        name="front",
    )(fir_taps.astype(jnp.float32), counts, records.reshape(rows, raw), jnp.asarray(forward_rows(seglen)))
    if not fast:
        white = white.reshape(2, devices, width, rows).transpose(1, 0, 2, 3)
        white = white.reshape(devices, 2 * width, rows)
    bands = lax.all_to_all(white, AXES, 0, 0, tiled=True)
    if fast:
        by_i, by_j = (jnp.asarray(t) for t in spread_tables(block, segs))
        spread = pltpu.VMEM((nsta, segs, groups * 2 * width, lanes), jnp.float32)
        stacked = pl.pallas_call(
            functools.partial(cross_kernel, groups, segs),
            out_shape=jax.ShapeDtypeStruct((devices, CAP // 2, 2 * width, 128), bf16),
            in_specs=[SMEM, SMEM, SMEM, VMEM, VMEM, VMEM],
            out_specs=VMEM,
            scratch_shapes=[
                spread,
                spread,
                pltpu.VMEM((2, 2 * width, lanes), jnp.float32),
                pltpu.SMEM((nsta * CAP,), jnp.int32),
                pltpu.SMEM((nsta,), jnp.int32),
            ],
            compiler_params=params,
            name="cross",
        )(owners, pair_blocks, counts, bands, by_i, by_j)
    else:
        stacked = cross_plain(bands, counts, pair_blocks, owners, nsta, groups, segs, width)
    moved = lax.all_to_all(stacked, AXES, 0, 0, tiled=True)
    if not fast:
        moved = moved.reshape(2 * nfreq, CAP * lanes // groups)
    return pl.pallas_call(
        last_kernel_halves if fast else last_kernel,
        out_shape=jax.ShapeDtypeStruct((CAP, NLAG, lanes // groups), jnp.float32),
        in_specs=[VMEM, VMEM],
        out_specs=VMEM,
        compiler_params=params,
        name="last",
    )(jnp.asarray(inverse_rows(seglen, NLAG, width)), moved)


def solution(mesh):
    in_specs = (P("sta", "seg", None), P(), P(), P(), P())
    out_specs = P("sta", None, "seg")
    return jax.shard_map(local, mesh=mesh, in_specs=in_specs, out_specs=out_specs, check_vma=False)
```

time: 369 us -> 55.1 us (0.15)
  blocking collectives: 96.6 us -> 17.8 us
  waiting for transfers between devices: 83.7 us -> 10.4 us
  matrix products: 69.1 us -> 0 us
  local copies, waits for them, and re-layouts: 73.2 us -> 4.77 us
  other arithmetic: 23.9 us -> 0.7 us
  between operations: 14.4 us -> 0.04 us
  Pallas kernels: 0 us -> 13.9 us
    all_to_all x1, blocking collectives: 96.6 us -> 17.8 us  [local(): moved = lax.all_to_all(stacked, AXES, 0, 0, tiled=True)]
    unnamed x2 -> x0, waiting for transfers between devices: 75.5 us -> none
    dot_general x7 -> x0, matrix products: 69.1 us -> none  [the longest x1 21.4 us: local(): jnp.einsum('rbw,wn->rbn', window, fir_matrix(fir_taps), preferred_element...]
    unnamed x22 -> x20, local copies, waits for them, and re-layouts: 19.1 us -> 3.66 us
    pallas_call x0 -> x3, Pallas kernels: none -> 13.9 us  [the longest x1 9.94 us: local(): pl.pallas_call(functools.partial(cross_kernel, groups, segs), out_shape=j...]
    another operation x3 -> x0, other arithmetic: 13.1 us -> none
    sub x1 -> x0, local copies, waits for them, and re-layouts: 11.9 us -> none  [cross_spectra(): imag_sum - jnp.einsum(form, left_real, right_imag, preferred_element_type...]
    add x1 -> x0, local copies, waits for them, and re-layouts: 11.9 us -> none  [cross_spectra(): real_sum + jnp.einsum(form, left_imag, right_imag, preferred_element_type...]
  transfers between devices with their start and end apart: 2 -> 1, of which waited for: 2 -> 1; matrix products, arithmetic and copies ran while one was open for 2% -> 0% of each run, Pallas kernels for 0% -> 0%
where the time goes in v1:
time: 55.1 us; the launch traced here: 54.9 us
  blocking collectives  17.8 us (32%)
  Pallas kernels  13.9 us (25%)
  waiting for transfers between devices  10.4 us (19%)
  starting transfers between devices  7.3 us (13%)
  local copies, waits for them, and re-layouts  4.77 us (9%)
  other arithmetic  0.7 us (1%)
    all_to_all x1, blocking collectives, local(): moved = lax.all_to_all(stacked, AXES, 0, 0, tiled=True)  17.8 us
    all_to_all x1, waiting for transfers between devices, local(): bands = lax.all_to_all(white, AXES, 0, 0, tiled=True)  10.4 us
    pallas_call x1, Pallas kernels, local(): pl.pallas_call(functools.partial(cross_kernel, groups, segs), out_shape=j...  9.94 us
    all_to_all x1, starting transfers between devices, local(): bands = lax.all_to_all(white, AXES, 0, 0, tiled=True)  7.3 us
    unnamed x20, local copies, waits for them, and re-layouts  3.66 us
    pallas_call x1, Pallas kernels, local(): pl.pallas_call(functools.partial(front_kernel, block, segs), out_shape=ja...  3.17 us
    pallas_call x1, local copies, waits for them, and re-layouts, local(): pl.pallas_call(last_kernel_halves if fast else last_kernel, out_shape=jax...  1.11 us
  transfers between devices with their start and end apart: 1, of which 1 were waited for; matrix products, arithmetic and copies ran while one was open for 0% of the time, Pallas kernels for 0%

profile of v1, /device:TPU:0, one launch (start us, length us, event | category | flops | bytes accessed | tf_op | source)
XLA Modules:
  0.0 54.9 jit_solution(10659103889364839780)
XLA Ops:
  0.0 0.0 copy-start.6
  0.0 0.0 copy-start.7
  0.0 0.0 copy-start.8
  0.0 0.7 %convert_element_type.3.taps_ref = f32[32]{0:T(128)S(1)} convert(bf16[32]{0:T(256)(128)(2,1)} %param.10) | non-fusion elementwise | flops 32 | bytes 192 | tf_op jit(solution)/shard_map/convert_element_type | solution.py:238
  0.7 0.0 copy-start
  0.7 1.6 %copy-done = bf16[1024,1024]{1,0:T(8,128)(2,1)S(1)} copy-done((bf16[1024,1024]{1,0:T(8,128)(2,1)S(1)}, bf16[1024,1024]{1,0:T(8,128)(2,1)}, u32[]{:S(2)}) %copy-start) | copy-done | bytes 2097176
  2.3 0.0 copy-start.1
  2.3 1.2 %copy-done.1 = bf16[16,8,4096]{2,1,0:T(8,128)(2,1)S(1)} copy-done((bf16[16,8,4096]{2,1,0:T(8,128)(2,1)S(1)}, bf16[16,8,4096]{2,1,0:T(8,128)(2,1)}, u32[]{:S(2)}) %copy-start.1) | copy-done | bytes 1048600
  3.5 0.0 copy-start.5
  3.5 0.7 %copy-done.5 = s32[128]{0:T(128)S(1)} copy-done((s32[128]{0:T(128)S(1)}, s32[128]{0:T(128)}, u32[]{:S(2)}) %copy-start.5) | copy-done | bytes 536
  4.2 0.0 copy-start.3
  4.2 0.0 copy-start.4
  4.2 3.2 %front.1 = bf16[32,32,128]{2,1,0:T(8,128)(2,1)} custom-call(f32[32]{0:T(128)S(1)} %convert_element_type.3.taps_ref, s32[128]{0:T(128)S(1)} %copy-done.5, bf16[128,4096]{1,0:T(8,128)(2,1)S(1)} %bitcast.1, bf16[1024,1024]{1,0:T(8,128)(2,1)S(1)} %copy-done), custom_call_target="tpu_custom_call" | custom-call | tf_op jit(solution)/shard_map/front/pallas_call | solution.py:230
  7.4 0.0 copy-start.2
  7.4 7.3 %all-to-all-start = ((bf16[32,32,128]{2,1,0:T(8,128)(2,1)}), bf16[32,32,128]{2,1,0:T(8,128)(2,1)S(1)}, u32[]{:S(2)}, u32[]{:S(2)}) async-start(bf16[32,32,128]{2,1,0:T(8,128)(2,1)} %front.1), calls=%async_computation | async-start | bytes 524288 | tf_op jit(solution)/shard_map/all_to_all | solution.py:242
  14.7 0.0 copy-done.7
  14.7 0.1 copy.11.pairs_ref
  14.8 0.0 copy-done.8
  14.8 0.1 copy.10.owners_ref
  14.8 10.4 %all-to-all-done.band_ref = bf16[32,32,128]{2,1,0:T(8,128)(2,1)S(1)} async-done(((bf16[32,32,128]{2,1,0:T(8,128)(2,1)}), bf16[32,32,128]{2,1,0:T(8,128)(2,1)S(1)}, u32[]{:S(2)}, u32[]{:S(2)}) %all-to-all-start) | async-done | bytes 262176 | tf_op jit(solution)/shard_map/all_to_all | solution.py:242
  25.3 0.0 copy-done.6
  25.3 0.0 copy-done.3
  25.3 0.0 copy-done.4
  25.3 9.9 %cross.1 = bf16[32,2,32,128]{3,2,1,0:T(8,128)(2,1)S(1)} custom-call(s32[16,1]{1,0:T(8,128)S(1)} %copy.10.owners_ref, s32[16,2]{1,0:T(8,128)S(1)} %copy.11.pairs_ref, s32[128]{0:T(128)S(1)} %copy-done.6, bf16[32,32,128]{2,1,0:T(8,128)(2,1)S(1)} %all-to-all-done.band_ref, bf16[128,2048]{1,0:T(8,128)(2,1)S(1)} %copy-done.4, bf16[128,2048]{1,0:T(8,128)(2,1)S(1)} %copy-done.3), custom_call_target="tpu_custom_call" | custom-call | tf_op jit(solution)/shard_map/cross/pallas_call | solution.py:246
  35.2 17.8 %all_to_all.10.stack_ref = bf16[32,2,32,128]{3,2,1,0:T(8,128)(2,1)S(1)} all-to-all(bf16[32,2,32,128]{3,2,1,0:T(8,128)(2,1)S(1)} %cross.1), channel_id=1, replica_groups=mesh['sta'=8,'seg'=4] {'sta','seg'}, dimensions={0} | all-to-all | bytes 1048576 | tf_op jit(solution)/shard_map/all_to_all | solution.py:263
  53.0 0.0 copy-done.2
  53.0 0.8 %last.1 = f32[4,512,64]{2,1,0:T(8,128)S(1)} custom-call(bf16[512,1024]{1,0:T(8,128)(2,1)S(1)} %copy-done.2, bf16[32,2,32,128]{3,2,1,0:T(8,128)(2,1)S(1)} %all_to_all.10.stack_ref), custom_call_target="tpu_custom_call" | custom-call | tf_op jit(solution)/shard_map/last/pallas_call | solution.py:266
  53.7 1.1 %copy.12 = f32[4,512,64]{1,2,0:T(8,128)} copy(f32[4,512,64]{2,1,0:T(8,128)S(1)} %last.1) | data formatting | bytes 1048576 | tf_op jit(solution)/shard_map/last/pallas_call | solution.py:266
Async XLA Ops:
  0.0 25.3 %copy-start.6 = (s32[128]{0:T(128)S(1)}, s32[128]{0:T(128)}, u32[]{:S(2)}) copy-start(s32[128]{0:T(128)} %counts_ref.3) | copy-start | bytes 1540
  0.0 14.7 %copy-start.7 = (s32[16,2]{0,1:T(2,128)S(1)}, s32[16,2]{0,1:T(2,128)}, u32[]{:S(2)}) copy-start(s32[16,2]{0,1:T(2,128)} %param.12) | copy-start | bytes 388
  0.0 14.8 %copy-start.8 = (s32[16,1]{0,1:T(1,128)S(1)}, s32[16,1]{0,1:T(1,128)}, u32[]{:S(2)}) copy-start(s32[16,1]{0,1:T(1,128)} %param.13) | copy-start | bytes 196
  0.7 1.6 %copy-start = (bf16[1024,1024]{1,0:T(8,128)(2,1)S(1)}, bf16[1024,1024]{1,0:T(8,128)(2,1)}, u32[]{:S(2)}) copy-start(bf16[1024,1024]{1,0:T(8,128)(2,1)} %constant.8.clone.dft_ref) | copy-start | bytes 6291460
  2.3 1.2 %copy-start.1 = (bf16[16,8,4096]{2,1,0:T(8,128)(2,1)S(1)}, bf16[16,8,4096]{2,1,0:T(8,128)(2,1)}, u32[]{:S(2)}) copy-start(bf16[16,8,4096]{2,1,0:T(8,128)(2,1)} %param.9) | copy-start | bytes 3145732
  3.5 0.7 %copy-start.5 = (s32[128]{0:T(128)S(1)}, s32[128]{0:T(128)}, u32[]{:S(2)}) copy-start(s32[128]{0:T(128)} %counts_ref.3) | copy-start | bytes 1540
  4.2 21.1 %copy-start.3 = (bf16[128,2048]{1,0:T(8,128)(2,1)S(1)}, bf16[128,2048]{1,0:T(8,128)(2,1)}, u32[]{:S(2)}) copy-start(bf16[128,2048]{1,0:T(8,128)(2,1)} %constant.10.clone.by_j_ref) | copy-start | bytes 1572868
  4.2 21.1 %copy-start.4 = (bf16[128,2048]{1,0:T(8,128)(2,1)S(1)}, bf16[128,2048]{1,0:T(8,128)(2,1)}, u32[]{:S(2)}) copy-start(bf16[128,2048]{1,0:T(8,128)(2,1)} %constant.9.clone.by_i_ref) | copy-start | bytes 1572868
  7.4 45.6 %copy-start.2 = (bf16[512,1024]{1,0:T(8,128)(2,1)S(1)}, bf16[512,1024]{1,0:T(8,128)(2,1)}, u32[]{:S(2)}) copy-start(bf16[512,1024]{1,0:T(8,128)(2,1)} %constant.11.clone.inv_ref) | copy-start | bytes 3145732
  7.4 17.9 %all-to-all-start = ((bf16[32,32,128]{2,1,0:T(8,128)(2,1)}), bf16[32,32,128]{2,1,0:T(8,128)(2,1)S(1)}, u32[]{:S(2)}, u32[]{:S(2)}) async-start(bf16[32,32,128]{2,1,0:T(8,128)(2,1)} %front.1), calls=%async_computation | async-start | bytes 524288 | tf_op jit(solution)/shard_map/all_to_all | solution.py:242
